TPU v7x, 128 devices: a whole 4x4x4 slice. The times are simulated.
128 devices in a mesh: tx: 8 (over x, core), ty: 16 (over z, y).
Axes of the slice: x: 4, y: 4, z: 4, core: 2. Of those that a mesh axis runs over, the one named last changes fastest.
Arguments:
- solution: float32 [4, 1024, 4096], P(None, 'tx', 'ty'), may hold values from -6 to 6
- residual: float32 [4, 1024, 4096], P(None, 'tx', 'ty')
- direction: float32 [4, 1024, 4096], P(None, 'tx', 'ty')
- blocks: bfloat16 [32768, 128, 256], P(('tx', 'ty')), may hold values from -0.375 to 0.375
- bin_owner: int32 [32768, 1], P(('tx', 'ty')), may hold values from 0 to 127; in each aligned block of 256 rows (0 to 255, 256 to 511, ...) at most 3 rows name the same one
- bin_tile: int32 [32768], P(('tx', 'ty')), may hold values from 0 to 127
Outputs:
- next_solution: float32 [4, 1024, 4096], P(None, 'tx', 'ty')
- next_residual: float32 [4, 1024, 4096], P(None, 'tx', 'ty')
- next_direction: float32 [4, 1024, 4096], P(None, 'tx', 'ty')
Inputs may be any that keep to these rules, and one draw needn't show every extreme that they name: `bin_owner`: among the bins of one device, at most 3 name the same owner, and on some devices some owner is named by exactly 3 of them.
All inputs are finite; a program needn't handle non-finite values.
Results may differ from a plain program's by a relative error of at most 0.0024.
Values may be sent and summed in bfloat16 or wider, within the bound.
A program may use at most 128 MiB of HBM per device.

v0:
```python
import jax
import jax.numpy as jnp
from jax import lax
from jax.sharding import PartitionSpec as P

TILE_SIDE = 16
smooth_weight = 0.25


def padded_2(shard, sides, width):
    for axis, dim in sides:
        size, length = (lax.axis_size(axis), shard.shape[dim])
        up = [(i, (i + 1) % size) for i in range(size - 1)]
        down = [(j, i) for i, j in up]
        last = lax.slice_in_dim(shard, length - width, length, axis=dim)
        initial = lax.slice_in_dim(shard, 0, width, axis=dim)
        before = lax.ppermute(last, axis, up)
        after = lax.ppermute(initial, axis, down)
        shard = jnp.concatenate([before, shard, after], axis=dim)
    return shard


def to_tiles(field):
    beacons, rows, cols = field.shape
    across = rows // TILE_SIDE
    down = cols // TILE_SIDE
    shaped = field.reshape(beacons, across, TILE_SIDE, down, TILE_SIDE).transpose(1, 3, 0, 2, 4)
    return shaped.reshape(across * down, beacons, TILE_SIDE * TILE_SIDE)


def to_field(tiles, rows, cols):
    beacons = tiles.shape[1]
    across = rows // TILE_SIDE
    down = cols // TILE_SIDE
    shaped = tiles.reshape(across, down, beacons, TILE_SIDE, TILE_SIDE).transpose(2, 0, 3, 1, 4)
    return shaped.reshape(beacons, rows, cols)


def laplace_local(field):
    padded = padded_2(field.astype(jnp.bfloat16), (("tx", 1), ("ty", 2)), 1).astype(field.dtype)
    near = padded[:, 2:, 1:-1] + padded[:, :-2, 1:-1] + padded[:, 1:-1, 2:] + padded[:, 1:-1, :-2]
    return 4.0 * field - near


def per_device(solution, residual, direction, blocks, bin_owner, bin_tile):
    beacons, rows, cols = direction.shape
    cells = TILE_SIDE * TILE_SIDE
    across_x = lax.axis_size("tx")
    across_y = lax.axis_size("ty")
    devices = across_x * across_y
    count = blocks.shape[0]
    cap = max(2, 3 * count // (2 * devices))
    owner = bin_owner[:, 0]
    member = (owner[:, None] == jnp.arange(devices, dtype=jnp.int32)[None, :]).astype(jnp.int32)
    before = jnp.cumsum(member, axis=0) - member
    rank = jnp.sum(before * member, axis=1)
    slot = owner * cap + rank
    request = jnp.full((devices * cap,), -1, jnp.int32).at[slot].set(bin_tile)
    wanted = lax.all_to_all(
        request.reshape(devices, cap), ("tx", "ty"), split_axis=0, concat_axis=0, tiled=True
    )
    wanted = jnp.maximum(wanted.reshape(devices * cap), 0)
    own_tiles = to_tiles(direction.astype(jnp.bfloat16))
    outgoing = jnp.take(own_tiles, wanted, axis=0)
    fetched = lax.all_to_all(
        outgoing.reshape(devices, cap, beacons, cells),
        ("tx", "ty"),
        split_axis=0,
        concat_axis=0,
        tiled=True,
    )
    fetched = fetched.reshape(devices * cap, beacons, cells)
    picked = jnp.take(fetched, slot, axis=0)
    samples = jnp.einsum("bsc,bkc->bks", blocks, picked, preferred_element_type=jnp.float32).astype(
        jnp.bfloat16
    )
    adjoint = jnp.einsum("bsc,bks->bkc", blocks, samples, preferred_element_type=jnp.float32)
    returned = jnp.zeros((devices * cap, beacons, cells), jnp.float32).at[slot].set(adjoint)
    arrived = lax.all_to_all(
        returned.reshape(devices, cap, beacons, cells),
        ("tx", "ty"),
        split_axis=0,
        concat_axis=0,
        tiled=True,
    )
    arrived = arrived.reshape(devices * cap, beacons, cells)
    data_tiles = jnp.zeros(own_tiles.shape, jnp.float32).at[wanted].add(arrived)
    image = to_field(data_tiles, rows, cols) + smooth_weight * laplace_local(direction)
    norm_old = lax.psum(jnp.sum(residual * residual, axis=(1, 2)), ("tx", "ty"))
    curvature = lax.psum(jnp.sum(direction * image, axis=(1, 2)), ("tx", "ty"))
    alpha = norm_old / curvature
    next_residual = residual - alpha[:, None, None] * image
    norm_new = lax.psum(jnp.sum(next_residual * next_residual, axis=(1, 2)), ("tx", "ty"))
    next_solution = solution + alpha[:, None, None] * direction
    next_direction = next_residual + (norm_new / norm_old)[:, None, None] * direction
    return (next_solution, next_residual, next_direction)


def solution(mesh):
    placed = (
        P(None, "tx", "ty"),
        P(None, "tx", "ty"),
        P(None, "tx", "ty"),
        P(("tx", "ty"), None, None),
        P(("tx", "ty"), None),
        P(("tx", "ty")),
    )
    return jax.shard_map(
        per_device,
        mesh=mesh,
        in_specs=placed,
        out_specs=(P(None, "tx", "ty"), P(None, "tx", "ty"), P(None, "tx", "ty")),
        check_vma=False,
    )
```

profile of v0, /device:TPU:1, one launch (start us, length us, event | category | flops | bytes accessed | tf_op | source)
XLA Modules:
  0.0 294.0 jit_solution(3272720926653905522)
XLA Ops:
  0.6 0.8 copy.23
  1.4 0.2 fusion.10
  1.7 0.9 fusion.12
  2.6 0.7 and_reduce_fusion
  3.3 1.6 scatter_custom_fusion
  4.8 0.8 all_to_all.12
  5.7 11.5 %all-to-all-start = ((s32[128,1,3]{2,1,0:T(1,128)}), s32[128,1,3]{2,1,0:T(1,128)S(1)}, u32[]{:S(2)}, u32[]{:S(2)}) async-start(s32[128,1,3]{2,1,0:T(1,128)} %bitcast.7), calls=%async_computation | async-start | bytes 131072 | tf_op jit(solution)/shard_map/all_to_all | solution.py:59
  17.2 1.1 convert_element_type.19
  18.3 2.5 reshape.85
  20.7 2.1 copy.33
  22.9 2.0 reshape.86
  24.9 0.2 copy.29
  25.1 1.8 all-to-all-done
  26.9 0.2 maximum_reduce_fusion
  27.1 0.2 reshape.126
  27.3 0.1 maximum_compare_fusion
  27.4 0.1 copy.26
  27.5 0.1 copy.27
  27.7 2.3 gather_fusion
  30.0 1.4 broadcast_select_fusion
  31.4 8.0 %all-to-all-start.1 = ((bf16[128,3,4,256]{3,2,1,0:T(4,128)(2,1)}), bf16[128,3,4,256]{3,2,1,0:T(4,128)(2,1)S(1)}, u32[]{:S(2)}, u32[]{:S(2)}) async-start(bf16[128,3,4,256]{3,2,1,0:T(4,128)(2,1)} %broadcast_select_fusion), calls=%async_computation.1 | async-start | bytes 1572864 | tf_op jit(solution)/shard_map/all_to_all | solution.py:65
  39.5 16.6 %all-to-all-done.1 = bf16[128,3,4,256]{3,2,1,0:T(4,128)(2,1)S(1)} async-done(((bf16[128,3,4,256]{3,2,1,0:T(4,128)(2,1)}), bf16[128,3,4,256]{3,2,1,0:T(4,128)(2,1)S(1)}, u32[]{:S(2)}, u32[]{:S(2)}) %all-to-all-start.1) | async-done | bytes 786464 | tf_op jit(solution)/shard_map/all_to_all | solution.py:65
  56.1 1.2 gather_fusion.1
  57.3 16.9 %fusion = f32[256,4,256]{2,1,0:T(4,128)S(1)} fusion(bf16[256,128,256]{2,1,0:T(8,128)(2,1)} %param.9, bf16[256,4,256]{2,1,0:T(4,128)(2,1)S(1)} %gather_fusion.1, pred[256]{0:T(512)(128)(4,1)S(1)} %get-tuple-element.9), kind=kOutput, calls=%fused_computation.8 | convolution fusion | flops 134610944 | bytes 18350336 | tf_op jit(solution)/shard_map/bsc,bks->bkc/dot_general | solution.py:77
  74.1 1.4 broadcast_in_dim.38
  75.5 23.9 %scatter_fusion = f32[384,4,256]{2,1,0:T(4,128)} fusion(f32[384,4,256]{2,1,0:T(4,128)} %broadcast_in_dim.38, s32[256]{0:T(256)S(1)} %bitcast.49, f32[256,4,256]{2,1,0:T(4,128)S(1)} %fusion), kind=kCustom, calls=%fused_computation.3 | custom fusion | bytes 3146752 | tf_op jit(solution)/shard_map/scatter | solution.py:78
  99.4 4.2 %all-to-all-start.2 = ((f32[128,3,4,256]{3,2,1,0:T(4,128)}), f32[128,3,4,256]{3,2,1,0:T(4,128)S(1)}, u32[]{:S(2)}, u32[]{:S(2)}) async-start(f32[128,3,4,256]{3,2,1,0:T(4,128)} %bitcast.12), calls=%async_computation.2 | async-start | bytes 3145728 | tf_op jit(solution)/shard_map/all_to_all | solution.py:79
  103.6 3.1 %collective-permute-start.1 = (bf16[4,1,256]{2,1,0:T(2,128)(2,1)S(1)}, bf16[4,1,256]{2,1,0:T(2,128)(2,1)S(1)}, u32[]{:S(2)}, u32[]{:S(2)}) collective-permute-start(bf16[4,1,256]{2,1,0:T(2,128)(2,1)S(1)} %get-tuple-element.16), channel_id=1, source_target_pairs={{16,0},{32,16},{48,32},{64,48},{80,64},{96,80},{112,96},{17,1},{33... | collective-permute-start | bytes 6152 | tf_op jit(solution)/shard_map/ppermute | solution.py:18
  106.7 2.4 collective-permute-start
  109.2 13.3 %collective-permute-done.1 = bf16[4,1,256]{2,1,0:T(2,128)(2,1)S(1)} collective-permute-done((bf16[4,1,256]{2,1,0:T(2,128)(2,1)S(1)}, bf16[4,1,256]{2,1,0:T(2,128)(2,1)S(1)}, u32[]{:S(2)}, u32[]{:S(2)}) %collective-permute-start.1) | collective-permute-done | bytes 2080 | tf_op jit(solution)/shard_map/ppermute | solution.py:18
  122.5 0.0 collective-permute-done
  122.5 0.1 pad_maximum_fusion
  122.5 0.1 fusion.20
  122.7 1.5 collective-permute-start.3
  124.1 4.0 %collective-permute-start.2 = (bf16[4,130,1]{2,1,0:T(8,128)(2,1)S(1)}, bf16[4,130,1]{2,1,0:T(8,128)(2,1)S(1)}, u32[]{:S(2)}, u32[]{:S(2)}) collective-permute-start(bf16[4,130,1]{2,1,0:T(8,128)(2,1)S(1)} %get-tuple-element.13), channel_id=1, source_target_pairs={{0,1},{1,2},{2,3},{3,4},{4,5},{5,6},{6,7},{7,8},{8,9},{9,10},{10,1... | collective-permute-start | bytes 3128 | tf_op jit(solution)/shard_map/ppermute | solution.py:17
  128.1 0.6 collective-permute-done.3
  128.8 1.4 collective-permute-done.2
  130.1 0.3 maximum_convert_fusion
  130.5 0.0 all-to-all-done.2
  130.5 0.1 broadcast_in_dim.36
  130.5 14.7 %scatter_fusion.1 = f32[128,4,256]{2,1,0:T(4,128)S(1)} fusion(f32[128,4,256]{2,1,0:T(4,128)S(1)} %broadcast_in_dim.36, s32[384]{0:T(512)S(1)} %reshape.126, f32[384,4,256]{2,1,0:T(4,128)S(1)} %bitcast.39), kind=kCustom, calls=%fused_computation.4 | custom fusion | flops 393216 | bytes 4720128 | tf_op jit(solution)/shard_map/scatter-add | solution.py:87
  145.2 0.1 copy.30
  145.3 2.6 reshape.90
  148.0 5.9 %copy.31 = f32[4,8,16,16,16]{4,3,2,1,0:T(8,128)} copy(f32[4,8,16,16,16]{4,2,3,1,0:T(8,128)} %bitcast.37) | data formatting | bytes 1048576 | tf_op jit(solution)/shard_map/transpose | solution.py:35
  153.8 0.0 copy-start
  153.8 0.0 copy-start.1
  153.8 3.6 %reshape.91 = f32[4,128,256]{2,1,0:T(8,128)S(1)} reshape(f32[4,8,16,16,16]{4,3,2,1,0:T(8,128)} %copy.31) | data formatting | bytes 1048576 | tf_op jit(solution)/shard_map/reshape | solution.py:36
  157.4 0.0 copy-done
  157.4 0.0 copy-done.1
  157.5 0.0 copy-start.3
  157.5 0.6 multiply_reduce_fusion.1
  158.0 72.0 %all-reduce = (f32[4]{0:T(128)S(1)}, f32[4]{0:T(128)S(1)}) all-reduce(f32[4]{0:T(128)S(1)} %get-tuple-element.17, f32[4]{0:T(128)S(1)} %get-tuple-element.7), channel_id=1, replica_groups=mesh['tx'=8,'ty'=16] {'tx','ty'}, use_global_device_ids=true, to_apply=%region_1.2 | all-reduce | flops 8 | bytes 64 | tf_op jit(solution)/shard_map/psum | solution.py:89
  230.1 0.2 multiply_reduce_fusion
  230.3 0.0 copy-start.2
  230.3 62.5 %psum.23 = f32[4]{0:T(128)S(1)} all-reduce(f32[4]{0:T(128)S(1)} %get-tuple-element.5), channel_id=1, replica_groups=mesh['tx'=8,'ty'=16] {'tx','ty'}, use_global_device_ids=true, to_apply=%region_11.12 | all-reduce | flops 4 | bytes 32 | tf_op jit(solution)/shard_map/psum | solution.py:93
  292.9 0.0 copy-done.3
  292.9 1.2 multiply_add_fusion
  294.0 0.0 copy-done.2
  (11 shorter events, 0.1 us)
Async XLA Ops:
  5.7 21.2 %all-to-all-start = ((s32[128,1,3]{2,1,0:T(1,128)}), s32[128,1,3]{2,1,0:T(1,128)S(1)}, u32[]{:S(2)}, u32[]{:S(2)}) async-start(s32[128,1,3]{2,1,0:T(1,128)} %bitcast.7), calls=%async_computation | async-start | bytes 131072 | tf_op jit(solution)/shard_map/all_to_all | solution.py:59
  31.4 24.7 %all-to-all-start.1 = ((bf16[128,3,4,256]{3,2,1,0:T(4,128)(2,1)}), bf16[128,3,4,256]{3,2,1,0:T(4,128)(2,1)S(1)}, u32[]{:S(2)}, u32[]{:S(2)}) async-start(bf16[128,3,4,256]{3,2,1,0:T(4,128)(2,1)} %broadcast_select_fusion), calls=%async_computation.1 | async-start | bytes 1572864 | tf_op jit(solution)/shard_map/all_to_all | solution.py:65
  99.4 31.1 %all-to-all-start.2 = ((f32[128,3,4,256]{3,2,1,0:T(4,128)}), f32[128,3,4,256]{3,2,1,0:T(4,128)S(1)}, u32[]{:S(2)}, u32[]{:S(2)}) async-start(f32[128,3,4,256]{3,2,1,0:T(4,128)} %bitcast.12), calls=%async_computation.2 | async-start | bytes 3145728 | tf_op jit(solution)/shard_map/all_to_all | solution.py:79
  103.6 18.9 %collective-permute-start.1 = (bf16[4,1,256]{2,1,0:T(2,128)(2,1)S(1)}, bf16[4,1,256]{2,1,0:T(2,128)(2,1)S(1)}, u32[]{:S(2)}, u32[]{:S(2)}) collective-permute-start(bf16[4,1,256]{2,1,0:T(2,128)(2,1)S(1)} %get-tuple-element.16), channel_id=1, source_target_pairs={{16,0},{32,16},{48,32},{64,48},{80,64},{96,80},{112,96},{17,1},{33... | collective-permute-start | bytes 6152 | tf_op jit(solution)/shard_map/ppermute | solution.py:18
  106.7 15.7 %collective-permute-start = (bf16[4,1,256]{2,1,0:T(2,128)(2,1)S(1)}, bf16[4,1,256]{2,1,0:T(2,128)(2,1)S(1)}, u32[]{:S(2)}, u32[]{:S(2)}) collective-permute-start(bf16[4,1,256]{2,1,0:T(2,128)(2,1)S(1)} %get-tuple-element.15), channel_id=1, source_target_pairs={{0,16},{16,32},{32,48},{48,64},{64,80},{80,96},{96,112},{1,17},{17... | collective-permute-start | bytes 6152 | tf_op jit(solution)/shard_map/ppermute | solution.py:17
  122.7 6.1 %collective-permute-start.3 = (bf16[4,130,1]{2,1,0:T(8,128)(2,1)S(1)}, bf16[4,130,1]{2,1,0:T(8,128)(2,1)S(1)}, u32[]{:S(2)}, u32[]{:S(2)}) collective-permute-start(bf16[4,130,1]{2,1,0:T(8,128)(2,1)S(1)} %get-tuple-element.14), channel_id=1, source_target_pairs={{1,0},{2,1},{3,2},{4,3},{5,4},{6,5},{7,6},{8,7},{9,8},{10,9},{11,1... | collective-permute-start | bytes 3128 | tf_op jit(solution)/shard_map/ppermute | solution.py:18
  124.1 6.0 %collective-permute-start.2 = (bf16[4,130,1]{2,1,0:T(8,128)(2,1)S(1)}, bf16[4,130,1]{2,1,0:T(8,128)(2,1)S(1)}, u32[]{:S(2)}, u32[]{:S(2)}) collective-permute-start(bf16[4,130,1]{2,1,0:T(8,128)(2,1)S(1)} %get-tuple-element.13), channel_id=1, source_target_pairs={{0,1},{1,2},{2,3},{3,4},{4,5},{5,6},{6,7},{7,8},{8,9},{9,10},{10,1... | collective-permute-start | bytes 3128 | tf_op jit(solution)/shard_map/ppermute | solution.py:17
  153.8 3.6 %copy-start = (f32[4,128,256]{2,1,0:T(8,128)S(1)}, f32[4,128,256]{2,1,0:T(8,128)}, u32[]{:S(2)}) copy-start(f32[4,128,256]{2,1,0:T(8,128)} %param.8) | copy-start | bytes 1572868
  153.8 3.6 %copy-start.1 = (f32[4,128,256]{2,1,0:T(8,128)S(1)}, f32[4,128,256]{2,1,0:T(8,128)}, u32[]{:S(2)}) copy-start(f32[4,128,256]{2,1,0:T(8,128)} %param.7) | copy-start | bytes 1572868
  157.5 135.4 %copy-start.3 = (f32[4,128,256]{2,1,0:T(8,128)S(1)}, f32[4,128,256]{2,1,0:T(8,128)}, u32[]{:S(2)}) copy-start(f32[4,128,256]{2,1,0:T(8,128)} %param.6) | copy-start | bytes 1572868
  230.3 63.7 %copy-start.2 = (f32[4,128,256]{2,1,0:T(8,128)}, f32[4,128,256]{2,1,0:T(8,128)S(1)}, u32[]{:S(2)}) copy-start(f32[4,128,256]{2,1,0:T(8,128)S(1)} %get-tuple-element.6) | copy-start | bytes 1572868
where the time goes:
time: 295 us; the launch traced here: 294 us
  blocking collectives  135 us (46%)
  local copies, waits for them, and re-layouts  51.6 us (17%)
  starting transfers between devices  34.7 us (12%)
  waiting for transfers between devices  33.7 us (11%)
  other arithmetic  21.7 us (7%)
  matrix products  16.9 us (6%)
    psum x1, blocking collectives, per_device(): norm_old = lax.psum(jnp.sum(residual * residual, axis=(1, 2)), ('tx', 'ty'))  72 us
    psum x1, blocking collectives, per_device(): lax.psum(jnp.sum(next_residual * next_residual, axis=(1, 2)), ('tx', 'ty'))  62.5 us
    scatter x1, local copies, waits for them, and re-layouts, per_device(): jnp.zeros((devices * cap, beacons, cells), jnp.float32).at[slot]  23.9 us
    dot_general x1, matrix products, per_device(): jnp.einsum('bsc,bks->bkc', blocks, samples, preferred_element_type=jnp.fl...  16.9 us
    all_to_all x1, waiting for transfers between devices, per_device(): lax.all_to_all(outgoing.reshape(devices, cap, beacons, cells), ('tx', 'ty...  16.6 us
    scatter-add x1, other arithmetic, per_device(): data_tiles = jnp.zeros(own_tiles.shape, jnp.float32).at[wanted].add(arrived)  14.7 us
    ppermute x2, waiting for transfers between devices, padded_2(): after = lax.ppermute(initial, axis, down)  13.9 us
    all_to_all x1, starting transfers between devices, per_device(): lax.all_to_all(request.reshape(devices, cap), ('tx', 'ty'), split_axis=0,...  11.5 us
  transfers between devices with their start and end apart: 7, of which 5 were waited for; matrix products, arithmetic and copies ran while one was open for 3% of the time, Pallas kernels for 0%

commit v1 on v0

--- a/solution.py
+++ b/solution.py
@@ -86,7 +86,12 @@
     arrived = arrived.reshape(devices * cap, beacons, cells)
     data_tiles = jnp.zeros(own_tiles.shape, jnp.float32).at[wanted].add(arrived)
     image = to_field(data_tiles, rows, cols) + smooth_weight * laplace_local(direction)
-    norm_old = lax.psum(jnp.sum(residual * residual, axis=(1, 2)), ("tx", "ty"))
+
+    def _edit_ladders(local_array):
+        long_array = jax.lax.all_gather(local_array, ("tx", "ty")).sum(axis=0)
+        return long_array
+
+    norm_old = _edit_ladders(jnp.sum(residual * residual, axis=(1, 2)))
     curvature = lax.psum(jnp.sum(direction * image, axis=(1, 2)), ("tx", "ty"))
     alpha = norm_old / curvature
     next_residual = residual - alpha[:, None, None] * image

time: 295 us -> 296 us (level)
    psum x1 -> x0, blocking collectives: 72 us -> none  [per_device(): norm_old = lax.psum(jnp.sum(residual * residual, axis=(1, 2)), ('tx', 'ty'))]
    unnamed x0 -> x1, blocking collectives: none -> 72 us
where the time goes in v1:
time: 296 us; the launch traced here: 294 us
  blocking collectives  135 us (46%)
  local copies, waits for them, and re-layouts  51.9 us (18%)
  starting transfers between devices  34.9 us (12%)
  waiting for transfers between devices  33.3 us (11%)
  other arithmetic  21.8 us (7%)
  matrix products  16.9 us (6%)
    unnamed x1, blocking collectives  72 us
    psum x1, blocking collectives, per_device(): lax.psum(jnp.sum(next_residual * next_residual, axis=(1, 2)), ('tx', 'ty'))  62.6 us
    scatter x1, local copies, waits for them, and re-layouts, per_device(): jnp.zeros((devices * cap, beacons, cells), jnp.float32).at[slot]  23.9 us
    dot_general x1, matrix products, per_device(): jnp.einsum('bsc,bks->bkc', blocks, samples, preferred_element_type=jnp.fl...  16.9 us
    all_to_all x1, waiting for transfers between devices, per_device(): lax.all_to_all(outgoing.reshape(devices, cap, beacons, cells), ('tx', 'ty...  16.6 us
    scatter-add x1, other arithmetic, per_device(): data_tiles = jnp.zeros(own_tiles.shape, jnp.float32).at[wanted].add(arrived)  14.7 us
    ppermute x2, waiting for transfers between devices, padded_2(): after = lax.ppermute(initial, axis, down)  13.5 us
    all_to_all x1, starting transfers between devices, per_device(): lax.all_to_all(request.reshape(devices, cap), ('tx', 'ty'), split_axis=0,...  11.5 us
  transfers between devices with their start and end apart: 7, of which 5 were waited for; matrix products, arithmetic and copies ran while one was open for 3% of the time, Pallas kernels for 0%

profile of v1, /device:TPU:1, one launch (start us, length us, event | category | flops | bytes accessed | tf_op | source)
XLA Modules:
  0.0 294.3 jit_solution(5105348849298314274)
XLA Ops:
  0.6 0.8 copy.23
  1.4 0.2 fusion.10
  1.7 0.9 fusion.12
  2.6 0.7 and_reduce_fusion
  3.3 1.6 scatter_custom_fusion
  4.8 0.8 all_to_all.12
  5.7 11.5 %all-to-all-start = ((s32[128,1,3]{2,1,0:T(1,128)}), s32[128,1,3]{2,1,0:T(1,128)S(1)}, u32[]{:S(2)}, u32[]{:S(2)}) async-start(s32[128,1,3]{2,1,0:T(1,128)} %bitcast.7), calls=%async_computation | async-start | bytes 131072 | tf_op jit(solution)/shard_map/all_to_all | solution.py:59
  17.2 1.1 convert_element_type.19
  18.3 2.5 reshape.85
  20.7 2.1 copy.33
  22.9 2.0 reshape.86
  24.9 0.2 copy.29
  25.1 1.8 all-to-all-done
  26.9 0.2 maximum_reduce_fusion
  27.1 0.2 reshape.126
  27.3 0.1 maximum_compare_fusion
  27.4 0.1 copy.26
  27.5 0.1 copy.27
  27.7 2.3 gather_fusion
  30.0 1.4 broadcast_select_fusion
  31.4 8.0 %all-to-all-start.1 = ((bf16[128,3,4,256]{3,2,1,0:T(4,128)(2,1)}), bf16[128,3,4,256]{3,2,1,0:T(4,128)(2,1)S(1)}, u32[]{:S(2)}, u32[]{:S(2)}) async-start(bf16[128,3,4,256]{3,2,1,0:T(4,128)(2,1)} %broadcast_select_fusion), calls=%async_computation.1 | async-start | bytes 1572864 | tf_op jit(solution)/shard_map/all_to_all | solution.py:65
  39.5 16.6 %all-to-all-done.1 = bf16[128,3,4,256]{3,2,1,0:T(4,128)(2,1)S(1)} async-done(((bf16[128,3,4,256]{3,2,1,0:T(4,128)(2,1)}), bf16[128,3,4,256]{3,2,1,0:T(4,128)(2,1)S(1)}, u32[]{:S(2)}, u32[]{:S(2)}) %all-to-all-start.1) | async-done | bytes 786464 | tf_op jit(solution)/shard_map/all_to_all | solution.py:65
  56.1 1.2 gather_fusion.1
  57.3 16.9 %fusion = f32[256,4,256]{2,1,0:T(4,128)S(1)} fusion(bf16[256,128,256]{2,1,0:T(8,128)(2,1)} %param.9, bf16[256,4,256]{2,1,0:T(4,128)(2,1)S(1)} %gather_fusion.1, pred[256]{0:T(512)(128)(4,1)S(1)} %get-tuple-element.9), kind=kOutput, calls=%fused_computation.8 | convolution fusion | flops 134610944 | bytes 18350336 | tf_op jit(solution)/shard_map/bsc,bks->bkc/dot_general | solution.py:77
  74.1 1.4 broadcast_in_dim.38
  75.5 23.9 %scatter_fusion = f32[384,4,256]{2,1,0:T(4,128)} fusion(f32[384,4,256]{2,1,0:T(4,128)} %broadcast_in_dim.38, s32[256]{0:T(256)S(1)} %bitcast.49, f32[256,4,256]{2,1,0:T(4,128)S(1)} %fusion), kind=kCustom, calls=%fused_computation.3 | custom fusion | bytes 3146752 | tf_op jit(solution)/shard_map/scatter | solution.py:78
  99.4 0.0 copy-start.2
  99.4 4.3 %all-to-all-start.2 = ((f32[128,3,4,256]{3,2,1,0:T(4,128)}), f32[128,3,4,256]{3,2,1,0:T(4,128)S(1)}, u32[]{:S(2)}, u32[]{:S(2)}) async-start(f32[128,3,4,256]{3,2,1,0:T(4,128)} %bitcast.12), calls=%async_computation.2 | async-start | bytes 3145728 | tf_op jit(solution)/shard_map/all_to_all | solution.py:79
  103.7 3.1 %collective-permute-start.1 = (bf16[4,1,256]{2,1,0:T(2,128)(2,1)S(1)}, bf16[4,1,256]{2,1,0:T(2,128)(2,1)S(1)}, u32[]{:S(2)}, u32[]{:S(2)}) collective-permute-start(bf16[4,1,256]{2,1,0:T(2,128)(2,1)S(1)} %get-tuple-element.16), channel_id=1, source_target_pairs={{16,0},{32,16},{48,32},{64,48},{80,64},{96,80},{112,96},{17,1},{33... | collective-permute-start | bytes 6152 | tf_op jit(solution)/shard_map/ppermute | solution.py:18
  106.9 2.4 collective-permute-start
  109.3 13.3 %collective-permute-done.1 = bf16[4,1,256]{2,1,0:T(2,128)(2,1)S(1)} collective-permute-done((bf16[4,1,256]{2,1,0:T(2,128)(2,1)S(1)}, bf16[4,1,256]{2,1,0:T(2,128)(2,1)S(1)}, u32[]{:S(2)}, u32[]{:S(2)}) %collective-permute-start.1) | collective-permute-done | bytes 2080 | tf_op jit(solution)/shard_map/ppermute | solution.py:18
  122.6 0.0 collective-permute-done
  122.6 0.1 pad_maximum_fusion
  122.7 0.1 fusion.20
  122.8 1.5 collective-permute-start.3
  124.3 4.0 %collective-permute-start.2 = (bf16[4,130,1]{2,1,0:T(8,128)(2,1)S(1)}, bf16[4,130,1]{2,1,0:T(8,128)(2,1)S(1)}, u32[]{:S(2)}, u32[]{:S(2)}) collective-permute-start(bf16[4,130,1]{2,1,0:T(8,128)(2,1)S(1)} %get-tuple-element.13), channel_id=1, source_target_pairs={{0,1},{1,2},{2,3},{3,4},{4,5},{5,6},{6,7},{7,8},{8,9},{9,10},{10,1... | collective-permute-start | bytes 3128 | tf_op jit(solution)/shard_map/ppermute | solution.py:17
  128.3 0.0 copy-done.2
  128.3 0.1 multiply_reduce_fusion.2
  128.4 0.2 dynamic-update-slice
  128.7 0.2 collective-permute-done.3
  128.9 1.4 collective-permute-done.2
  130.3 0.3 maximum_convert_fusion
  130.6 0.0 all-to-all-done.2
  130.6 0.1 broadcast_in_dim.36
  130.7 14.7 %scatter_fusion.1 = f32[128,4,256]{2,1,0:T(4,128)S(1)} fusion(f32[128,4,256]{2,1,0:T(4,128)S(1)} %broadcast_in_dim.36, s32[384]{0:T(512)S(1)} %reshape.126, f32[384,4,256]{2,1,0:T(4,128)S(1)} %bitcast.39), kind=kCustom, calls=%fused_computation.4 | custom fusion | flops 393216 | bytes 4720128 | tf_op jit(solution)/shard_map/scatter-add | solution.py:87
  145.4 0.1 copy.30
  145.5 2.6 reshape.90
  148.1 5.9 %copy.31 = f32[4,8,16,16,16]{4,3,2,1,0:T(8,128)} copy(f32[4,8,16,16,16]{4,2,3,1,0:T(8,128)} %bitcast.37) | data formatting | bytes 1048576 | tf_op jit(solution)/shard_map/transpose | solution.py:35
  154.0 0.0 copy-start
  154.0 3.5 %reshape.91 = f32[4,128,256]{2,1,0:T(8,128)S(1)} reshape(f32[4,8,16,16,16]{4,3,2,1,0:T(8,128)} %copy.31) | data formatting | bytes 1048576 | tf_op jit(solution)/shard_map/reshape | solution.py:36
  157.5 0.0 copy-done
  157.5 0.0 copy-start.3
  157.6 0.0 copy-start.4
  157.6 0.6 multiply_reduce_fusion.1
  158.1 72.0 %all-reduce.1 = (f32[512]{0:T(512)S(1)}, f32[4]{0:T(128)S(1)}) all-reduce(f32[512]{0:T(512)S(1)} %dynamic-update-slice, f32[4]{0:T(128)S(1)} %get-tuple-element.7), channel_id=2, replica_groups=mesh['tx'=8,'ty'=16] {'tx','ty'}, use_global_device_ids=true, to_apply=%add | all-reduce | flops 516 | bytes 4128
  230.2 0.1 reshape.132
  230.3 0.0 copy-done.3
  230.3 0.2 multiply_reduce_fusion
  230.6 0.0 copy-start.1
  230.6 62.6 %psum.15 = f32[4]{0:T(128)S(1)} all-reduce(f32[4]{0:T(128)S(1)} %get-tuple-element.5), channel_id=1, replica_groups=mesh['tx'=8,'ty'=16] {'tx','ty'}, use_global_device_ids=true, to_apply=%region_11.12 | all-reduce | flops 4 | bytes 32 | tf_op jit(solution)/shard_map/psum | solution.py:98
  293.2 0.0 copy-done.4
  293.2 1.2 multiply_add_fusion
  294.3 0.0 copy-done.1
  (13 shorter events, 0.1 us)
Async XLA Ops:
  5.7 21.2 %all-to-all-start = ((s32[128,1,3]{2,1,0:T(1,128)}), s32[128,1,3]{2,1,0:T(1,128)S(1)}, u32[]{:S(2)}, u32[]{:S(2)}) async-start(s32[128,1,3]{2,1,0:T(1,128)} %bitcast.7), calls=%async_computation | async-start | bytes 131072 | tf_op jit(solution)/shard_map/all_to_all | solution.py:59
  31.4 24.7 %all-to-all-start.1 = ((bf16[128,3,4,256]{3,2,1,0:T(4,128)(2,1)}), bf16[128,3,4,256]{3,2,1,0:T(4,128)(2,1)S(1)}, u32[]{:S(2)}, u32[]{:S(2)}) async-start(bf16[128,3,4,256]{3,2,1,0:T(4,128)(2,1)} %broadcast_select_fusion), calls=%async_computation.1 | async-start | bytes 1572864 | tf_op jit(solution)/shard_map/all_to_all | solution.py:65
  99.4 28.9 %copy-start.2 = (f32[4,128,256]{2,1,0:T(8,128)S(1)}, f32[4,128,256]{2,1,0:T(8,128)}, u32[]{:S(2)}) copy-start(f32[4,128,256]{2,1,0:T(8,128)} %param.7) | copy-start | bytes 1572868
  99.4 31.2 %all-to-all-start.2 = ((f32[128,3,4,256]{3,2,1,0:T(4,128)}), f32[128,3,4,256]{3,2,1,0:T(4,128)S(1)}, u32[]{:S(2)}, u32[]{:S(2)}) async-start(f32[128,3,4,256]{3,2,1,0:T(4,128)} %bitcast.12), calls=%async_computation.2 | async-start | bytes 3145728 | tf_op jit(solution)/shard_map/all_to_all | solution.py:79
  103.7 18.9 %collective-permute-start.1 = (bf16[4,1,256]{2,1,0:T(2,128)(2,1)S(1)}, bf16[4,1,256]{2,1,0:T(2,128)(2,1)S(1)}, u32[]{:S(2)}, u32[]{:S(2)}) collective-permute-start(bf16[4,1,256]{2,1,0:T(2,128)(2,1)S(1)} %get-tuple-element.16), channel_id=1, source_target_pairs={{16,0},{32,16},{48,32},{64,48},{80,64},{96,80},{112,96},{17,1},{33... | collective-permute-start | bytes 6152 | tf_op jit(solution)/shard_map/ppermute | solution.py:18
  106.9 15.7 %collective-permute-start = (bf16[4,1,256]{2,1,0:T(2,128)(2,1)S(1)}, bf16[4,1,256]{2,1,0:T(2,128)(2,1)S(1)}, u32[]{:S(2)}, u32[]{:S(2)}) collective-permute-start(bf16[4,1,256]{2,1,0:T(2,128)(2,1)S(1)} %get-tuple-element.15), channel_id=1, source_target_pairs={{0,16},{16,32},{32,48},{48,64},{64,80},{80,96},{96,112},{1,17},{17... | collective-permute-start | bytes 6152 | tf_op jit(solution)/shard_map/ppermute | solution.py:17
  122.8 6.1 %collective-permute-start.3 = (bf16[4,130,1]{2,1,0:T(8,128)(2,1)S(1)}, bf16[4,130,1]{2,1,0:T(8,128)(2,1)S(1)}, u32[]{:S(2)}, u32[]{:S(2)}) collective-permute-start(bf16[4,130,1]{2,1,0:T(8,128)(2,1)S(1)} %get-tuple-element.14), channel_id=1, source_target_pairs={{1,0},{2,1},{3,2},{4,3},{5,4},{6,5},{7,6},{8,7},{9,8},{10,9},{11,1... | collective-permute-start | bytes 3128 | tf_op jit(solution)/shard_map/ppermute | solution.py:18
  124.3 6.0 %collective-permute-start.2 = (bf16[4,130,1]{2,1,0:T(8,128)(2,1)S(1)}, bf16[4,130,1]{2,1,0:T(8,128)(2,1)S(1)}, u32[]{:S(2)}, u32[]{:S(2)}) collective-permute-start(bf16[4,130,1]{2,1,0:T(8,128)(2,1)S(1)} %get-tuple-element.13), channel_id=1, source_target_pairs={{0,1},{1,2},{2,3},{3,4},{4,5},{5,6},{6,7},{7,8},{8,9},{9,10},{10,1... | collective-permute-start | bytes 3128 | tf_op jit(solution)/shard_map/ppermute | solution.py:17
  154.0 3.6 %copy-start = (f32[4,128,256]{2,1,0:T(8,128)S(1)}, f32[4,128,256]{2,1,0:T(8,128)}, u32[]{:S(2)}) copy-start(f32[4,128,256]{2,1,0:T(8,128)} %param.8) | copy-start | bytes 1572868
  157.5 72.8 %copy-start.3 = (f32[4,128,256]{2,1,0:T(8,128)S(1)}, f32[4,128,256]{2,1,0:T(8,128)}, u32[]{:S(2)}) copy-start(f32[4,128,256]{2,1,0:T(8,128)} %param.7) | copy-start | bytes 1572868
  157.6 135.6 %copy-start.4 = (f32[4,128,256]{2,1,0:T(8,128)S(1)}, f32[4,128,256]{2,1,0:T(8,128)}, u32[]{:S(2)}) copy-start(f32[4,128,256]{2,1,0:T(8,128)} %param.6) | copy-start | bytes 1572868
  230.6 63.8 %copy-start.1 = (f32[4,128,256]{2,1,0:T(8,128)}, f32[4,128,256]{2,1,0:T(8,128)S(1)}, u32[]{:S(2)}) copy-start(f32[4,128,256]{2,1,0:T(8,128)S(1)} %get-tuple-element.6) | copy-start | bytes 1572868
